TPU v7x, 32 devices: a whole 2x2x4 slice. The times are simulated.
32 devices in a mesh: section: 2 (over x), dp: 4 (over z), tensor: 4 (over y, core).
Axes of the slice: x: 2, y: 2, z: 4, core: 2. Of those that a mesh axis runs over, the one named last changes fastest.
Arguments:
- block_input: bfloat16 [3840, 2048], P('dp'), may hold values from -6 to 6
- out_grad: bfloat16 [3840, 2048], P('dp'), may hold values from -6 to 6
- seq_lengths: int32 [4, 4], P('dp'), may hold values from 0 to 960, as said below
- attn_gains: bfloat16 [2, 2048], P('section'), may hold values from 0.099609375 to 1.8984375
- attn_weights: bfloat16 [2, 2, 2048, 2048], P('section', None, None, 'tensor')
- ffn_gain: bfloat16 [2048], replicated, may hold values from 0.099609375 to 1.8984375
- gate_weight: bfloat16 [2048, 5504], P(None, ('section', 'tensor')), may hold values from -0.125 to 0.125
- up_weight: bfloat16 [2048, 5504], P(None, ('section', 'tensor')), may hold values from -0.125 to 0.125
- down_weight: bfloat16 [5504, 2048], P(('section', 'tensor')), may hold values from -0.078125 to 0.078125
Outputs:
- block_output: bfloat16 [3840, 2048], P('dp', ('section', 'tensor'))
- input_grad: bfloat16 [3840, 2048], P('dp', ('section', 'tensor'))
- attn_gains_grad: float32 [2, 2048], P('section')
- attn_weights_grad: float32 [2, 2, 2048, 2048], P('section', None, None, 'tensor')
- ffn_gain_grad: float32 [2048], replicated
- gate_weight_grad: float32 [2048, 5504], P(None, ('section', 'tensor'))
- up_weight_grad: float32 [2048, 5504], P(None, ('section', 'tensor'))
- down_weight_grad: float32 [5504, 2048], P(('section', 'tensor'))
- activation_rms: float32 [2], replicated
Inputs may be any that keep to these rules, and one draw needn't show every extreme that they name: `seq_lengths`: row g lists the lengths of group g's sequences, packed in order from the group's first token slot: 1 to 4 positive entries first, zeros after, summing to at most 960; slots past the sum are padding. Some row holds one sequence of 960.
All inputs are finite; a program needn't handle non-finite values.
Results may differ from a plain program's by a relative error of at most 0.017.
Values may be sent and summed in bfloat16 or wider, within the bound.
No kernel may reach another device: no remote copies, remote signals or barrier semaphores. Data moves between devices by JAX's collectives and lax.ppermute only.
A program may use at most 256 MiB of HBM per device.

v0:
```python
import jax
import jax.numpy as jnp
from jax import lax
from jax.sharding import PartitionSpec as P

HEAD_SIZE = 128
epsilon = 1e-06
negative = -1e30


def spread(value, axis, source):
    kept = jnp.where(lax.axis_index(axis) == source, value, 0).astype(value.dtype)
    return lax.psum(kept, axis)


def passed_along(value, axis, steps):
    count = lax.axis_size(axis)
    initial, last = (max(0, -steps), min(count, count - steps))
    return lax.ppermute(value, axis, [(source, source + steps) for source in range(initial, last)])


def segment_ids(length_row, tok_count):
    seq_ends = jnp.cumsum(length_row)
    places = jnp.arange(tok_count, dtype=jnp.int32)
    return jnp.sum((places[:, None] >= seq_ends[None, :]).astype(jnp.int32), axis=1)


def norm_back(source, inverse, gain_vec, grad_in):
    scaled = grad_in * gain_vec
    inner_mean = jnp.mean(scaled * source, axis=-1, keepdims=True)
    return inverse * scaled - source * inverse**3 * inner_mean


def contract_rows(left_mat, right_mat):
    return lax.dot_general(
        left_mat, right_mat, (((0,), (0,)), ((), ())), preferred_element_type=jnp.float32
    )


def contract_cols(left_mat, right_mat):
    return lax.dot_general(
        left_mat, right_mat, (((1,), (1,)), ((), ())), preferred_element_type=jnp.float32
    )


def block_size(tok_count):
    size_rows = tok_count
    while size_rows > 1024 and size_rows % 2 == 0:
        size_rows = size_rows // 2
    return size_rows


def masked_scores(q_block, k_heads, seg_ids):
    score_scale = q_block.shape[2] ** (-0.5)
    scores = (
        jnp.einsum("qhd,khd->hqk", q_block, k_heads, preferred_element_type=jnp.float32)
        * score_scale
    )
    places = jnp.arange(seg_ids.shape[0], dtype=jnp.int32)
    allowed = (seg_ids[:, None] == seg_ids[None, :]) & (places[None, :] <= places[:, None])
    return jnp.where(allowed[None], scores, negative)


def attend_forward(queries, keys, values, seg_ids, head_dim):
    tok_count = queries.shape[0]
    heads_local = queries.shape[1] // head_dim
    q_heads = queries.reshape(tok_count, heads_local, head_dim)
    k_heads = keys.reshape(tok_count, heads_local, head_dim)
    v_heads = values.reshape(tok_count, heads_local, head_dim)
    block_rows = block_size(tok_count)
    scores = masked_scores(q_heads, k_heads, seg_ids)
    maximum = jnp.max(scores, axis=-1, keepdims=True)
    exponent = jnp.exp(scores - maximum)
    row_total = jnp.sum(exponent, axis=-1, keepdims=True)
    probs_low = (exponent / row_total).astype(jnp.bfloat16)
    block_out = jnp.einsum("hqk,khd->qhd", probs_low, v_heads, preferred_element_type=jnp.float32)
    outputs = [block_out.astype(jnp.bfloat16).reshape(block_rows, heads_local * head_dim)]
    lse_parts = [(maximum + jnp.log(row_total))[..., 0]]
    return (jnp.concatenate(outputs, axis=0), jnp.concatenate(lse_parts, axis=1))


def attend_backward(queries, keys, values, grad_out, seg_ids, log_total, head_dim):
    tok_count = queries.shape[0]
    heads_local = queries.shape[1] // head_dim
    score_scale = head_dim ** (-0.5)
    q_heads = queries.reshape(tok_count, heads_local, head_dim)
    k_heads = keys.reshape(tok_count, heads_local, head_dim)
    v_heads = values.reshape(tok_count, heads_local, head_dim)
    g_heads = grad_out.reshape(tok_count, heads_local, head_dim)
    block_rows = block_size(tok_count)
    grad_keys = jnp.zeros((tok_count, heads_local, head_dim), jnp.float32)
    grad_values = jnp.zeros((tok_count, heads_local, head_dim), jnp.float32)
    scores = masked_scores(q_heads, k_heads, seg_ids)
    prob_rows = jnp.exp(scores - log_total[:, 0:block_rows, None])
    probs_low = prob_rows.astype(jnp.bfloat16)
    grad_probs = jnp.einsum("qhd,khd->hqk", g_heads, v_heads, preferred_element_type=jnp.float32)
    inner_sum = jnp.sum(prob_rows * grad_probs, axis=-1, keepdims=True)
    grad_scores = (prob_rows * (grad_probs - inner_sum)).astype(jnp.bfloat16)
    block_q = (
        jnp.einsum("hqk,khd->qhd", grad_scores, k_heads, preferred_element_type=jnp.float32)
        * score_scale
    )
    grad_queries = [block_q]
    grad_keys = (
        grad_keys
        + jnp.einsum("hqk,qhd->khd", grad_scores, q_heads, preferred_element_type=jnp.float32)
        * score_scale
    )
    grad_values = grad_values + jnp.einsum(
        "hqk,qhd->khd", probs_low, g_heads, preferred_element_type=jnp.float32
    )
    flat_width = heads_local * head_dim
    query_grad = (
        jnp.concatenate(grad_queries, axis=0).reshape(tok_count, flat_width).astype(jnp.bfloat16)
    )
    kv_grad = jnp.stack(
        [grad_keys.reshape(tok_count, flat_width), grad_values.reshape(tok_count, flat_width)]
    ).astype(jnp.bfloat16)
    return (query_grad, kv_grad)


def shards(
    block_input,
    out_grad,
    seq_lengths,
    attn_gains,
    attn_weights,
    ffn_gain,
    gate_weight,
    up_weight,
    down_weight,
):
    tok_count, model_width = block_input.shape
    head_dim = HEAD_SIZE
    section_pos = lax.axis_index("section")
    is_first = section_pos == 0
    group_count = lax.axis_size("section") * lax.axis_size("tensor")
    share_part = 1.0 / group_count
    column_pos = section_pos * lax.axis_size("tensor") + lax.axis_index("tensor")
    columns = model_width // group_count
    col_start = column_pos * columns
    seg_ids = segment_ids(seq_lengths[0], tok_count)
    is_valid = (seg_ids < seq_lengths.shape[1]).astype(jnp.float32)[:, None]
    inputs_f = block_input.astype(jnp.float32)
    inverse = lax.rsqrt(jnp.mean(inputs_f * inputs_f, axis=-1, keepdims=True) + epsilon)
    gain_row = attn_gains[0].astype(jnp.float32)
    normed = (inputs_f * inverse * gain_row).astype(jnp.bfloat16)
    w_first = attn_weights[0, 0]
    w_second = attn_weights[0, 1]
    projected = jnp.dot(normed, w_first, preferred_element_type=jnp.float32).astype(jnp.bfloat16)
    second_proj = lax.cond(
        is_first,
        lambda: jnp.dot(normed, w_second, preferred_element_type=jnp.float32).astype(jnp.bfloat16),
        lambda: jnp.zeros_like(projected),
    )
    shared_kv = spread(jnp.stack([projected, second_proj]), "section", 0)
    heads_local = projected.shape[1] // head_dim
    attn_out, log_total = lax.cond(
        is_first,
        lambda: (jnp.zeros_like(projected), jnp.zeros((heads_local, tok_count), jnp.float32)),
        lambda: attend_forward(projected, shared_kv[0], shared_kv[1], seg_ids, head_dim),
    )
    partial_branch = lax.cond(
        is_first,
        lambda: jnp.zeros((tok_count, model_width), jnp.float32),
        lambda: contract_cols(attn_out, w_second),
    )
    gain_ffn = ffn_gain.astype(jnp.float32)
    branch = lax.psum(partial_branch, ("section", "tensor"))
    residual = inputs_f + branch
    resid_inv = lax.rsqrt(jnp.mean(residual * residual, axis=-1, keepdims=True) + epsilon)
    hidden_in = (residual * resid_inv * gain_ffn).astype(jnp.bfloat16)
    branch_cols = lax.dynamic_slice_in_dim(branch, col_start, columns, 1)
    resid_before = residual * share_part
    resid_after = 0.0
    gate_act = jnp.dot(hidden_in, gate_weight, preferred_element_type=jnp.float32)
    up_act = jnp.dot(hidden_in, up_weight, preferred_element_type=jnp.float32)
    gate_sig = jax.nn.sigmoid(gate_act)
    silu_val = gate_act * gate_sig
    hidden = (silu_val * up_act).astype(jnp.bfloat16)
    ffn_part = jnp.dot(hidden, down_weight, preferred_element_type=jnp.float32)
    output_sum = (
        lax.psum_scatter(
            (ffn_part + resid_before).astype(jnp.bfloat16),
            ("section", "tensor"),
            scatter_dimension=1,
            tiled=True,
        ).astype(jnp.float32)
        + resid_after
    )
    block_output = output_sum.astype(jnp.bfloat16)
    output_sq = jnp.sum(output_sum * output_sum * is_valid)
    branch_sq = jnp.sum(branch_cols * branch_cols * is_valid)
    count_term = jnp.where(column_pos == 0, jnp.sum(seq_lengths).astype(jnp.float32), 0.0)
    grad_hidden = contract_cols(out_grad, down_weight)
    grad_up = (grad_hidden * silu_val).astype(jnp.bfloat16)
    grad_gate = (grad_hidden * up_act * gate_sig * (1.0 + gate_act * (1.0 - gate_sig))).astype(
        jnp.bfloat16
    )
    down_grad = contract_rows(hidden, out_grad)
    gate_grad = contract_rows(hidden_in, grad_gate)
    up_grad = contract_rows(hidden_in, grad_up)
    grad_hidden_in = contract_cols(grad_gate, gate_weight) + contract_cols(grad_up, up_weight)
    ffn_gain_term = jnp.sum(grad_hidden_in * residual * resid_inv, axis=0)
    resid_part = norm_back(residual, resid_inv, gain_ffn, grad_hidden_in)
    grad_residual = out_grad.astype(jnp.float32) + lax.psum(resid_part, ("section", "tensor"))
    grad_branch_low = grad_residual.astype(jnp.bfloat16)
    grad_before = grad_residual * share_part
    grad_after = 0.0

    def cross_backward():
        grad_attn_out = jnp.dot(
            grad_branch_low, w_second, preferred_element_type=jnp.float32
        ).astype(jnp.bfloat16)
        return attend_backward(
            projected, shared_kv[0], shared_kv[1], grad_attn_out, seg_ids, log_total, head_dim
        )

    query_grad, kv_grad = lax.cond(
        is_first, lambda: (jnp.zeros_like(projected), jnp.zeros_like(shared_kv)), cross_backward
    )
    returned = passed_along(kv_grad, "section", -1)
    first_grad = jnp.where(is_first, returned[0], query_grad)
    left_second = jnp.where(is_first, normed, grad_branch_low)
    right_second = jnp.where(is_first, returned[1], attn_out)
    w_first_grad = contract_rows(normed, first_grad)
    w_second_grad = contract_rows(left_second, right_second)
    grad_normed = contract_cols(first_grad, w_first)
    grad_normed = grad_normed + lax.cond(
        is_first,
        lambda: contract_cols(returned[1], w_second),
        lambda: jnp.zeros((tok_count, model_width), jnp.float32),
    )
    attn_gain_term = jnp.sum(grad_normed * inputs_f * inverse, axis=0)
    input_part = norm_back(inputs_f, inverse, gain_row, grad_normed) + grad_before
    input_sum = (
        lax.psum_scatter(
            input_part.astype(jnp.bfloat16), ("section", "tensor"), scatter_dimension=1, tiled=True
        ).astype(jnp.float32)
        + grad_after
    )
    input_grad = input_sum.astype(jnp.bfloat16)
    attn_weight_grad = jnp.stack([w_first_grad, w_second_grad])[None]
    attn_weight_grad, gate_grad, up_grad, down_grad = (
        lax.psum(attn_weight_grad.astype(jnp.bfloat16), "dp").astype(jnp.float32),
        lax.psum(gate_grad.astype(jnp.bfloat16), "dp").astype(jnp.float32),
        lax.psum(up_grad.astype(jnp.bfloat16), "dp").astype(jnp.float32),
        lax.psum(down_grad.astype(jnp.bfloat16), "dp").astype(jnp.float32),
    )
    section_rows = jnp.where(
        jnp.arange(2, dtype=jnp.int32)[:, None] == section_pos, attn_gain_term[None, :], 0.0
    )
    gain_terms = jnp.concatenate([section_rows, ffn_gain_term[None, :]], axis=0)
    stat_terms = jnp.stack([output_sq, branch_sq, count_term])
    summed_gains, summed_stats = lax.psum((gain_terms, stat_terms), ("section", "dp", "tensor"))
    attn_gain_grad = lax.dynamic_slice_in_dim(summed_gains, section_pos, 1, 0)
    ffn_gain_grad = summed_gains[2]
    activation_rms = jnp.sqrt(summed_stats[:2] / (summed_stats[2] * model_width))
    return (
        block_output,
        input_grad,
        attn_gain_grad,
        attn_weight_grad,
        ffn_gain_grad,
        gate_grad,
        up_grad,
        down_grad,
        activation_rms,
    )


def solution(mesh):
    placed = (
        P("dp", None),
        P("dp", None),
        P("dp", None),
        P("section", None),
        P("section", None, None, "tensor"),
        P(),
        P(None, ("section", "tensor")),
        P(None, ("section", "tensor")),
        P(("section", "tensor"), None),
    )
    return jax.shard_map(
        shards,
        mesh=mesh,
        in_specs=placed,
        out_specs=(
            P("dp", ("section", "tensor")),
            P("dp", ("section", "tensor")),
            P("section", None),
            P("section", None, None, "tensor"),
            P(),
            P(None, ("section", "tensor")),
            P(None, ("section", "tensor")),
            P(("section", "tensor"), None),
            P(),
        ),
        check_vma=False,
    )
```

profile of v0, /device:TPU:0, one launch (start us, length us, event | category | flops | bytes accessed | tf_op | source)
XLA Modules:
  0.0 1044.1 jit_solution(1023561082317554751)
XLA Ops:
  19.4 4.7 conditional.5
  19.4 4.7 fusion
  27.5 61.7 %all-reduce.7.cloned.1.call-done = bf16[2,960,512]{2,1,0:T(8,128)(2,1)} async-done(((bf16[2,960,512]{2,1,0:T(8,128)(2,1)}), bf16[2,960,512]{2,1,0:T(8,128)(2,1)}) %all-reduce.7.cloned.1.call-update) | async-done | bytes 1966096 | tf_op jit(solution)/shard_map/psum | solution.py:13
  89.2 8.0 conditional.6
  102.1 156.3 %all-reduce.9.cloned.1.call-done = f32[960,2048]{1,0:T(8,128)} async-done(((f32[960,2048]{1,0:T(8,128)}), f32[960,2048]{1,0:T(8,128)}) %all-reduce.9.cloned.1.call-update) | async-done | bytes 7864336 | tf_op jit(solution)/shard_map/psum | solution.py:169
  258.4 5.4 multiply_reduce_fusion.3
  264.6 7.2 fusion.81
  276.5 6.9 multiply_convert_fusion.4
  283.5 5.5 fusion.83
  289.0 7.5 multiply_reduce_fusion.1
  300.5 7.3 add_convert_fusion
  307.9 114.6 %all-reduce.11.cloned.1.call-done = f32[960,2048]{1,0:T(8,128)} async-done(((f32[960,2048]{1,0:T(8,128)}), f32[960,2048]{1,0:T(8,128)}) %all-reduce.11.cloned.1.call-update) | async-done | bytes 7864336 | tf_op jit(solution)/shard_map/psum | solution.py:206
  422.5 7.8 fusion.51
  430.4 8.3 conditional.8
  440.3 7.9 convolution_convert_fusion.2
  457.1 87.8 %collective-permute-done = bf16[2,960,512]{2,1,0:T(8,128)(2,1)S(1)} collective-permute-done((bf16[2,960,512]{2,1,0:T(8,128)(2,1)S(1)}, bf16[2,960,512]{2,1,0:T(8,128)(2,1)S(1)}, u32[]{:S(2)}, u32[]{:S(2)}) %collective-permute-start) | collective-permute-done | bytes 1966112 | tf_op jit(solution)/shard_map/ppermute | solution.py:19
  554.4 7.0 conditional.9
  554.6 6.8 fusion.38
  561.4 8.6 fusion.50
  570.1 7.0 fusion.47
  582.8 44.1 %all-reduce = (f32[3,2048]{1,0:T(4,128)S(1)}, f32[3]{0:T(128)S(1)}) all-reduce(f32[3,2048]{1,0:T(4,128)S(1)} %pad_maximum_fusion.2, f32[3]{0:T(128)S(1)} %pad_maximum_fusion.3), channel_id=1, replica_groups=mesh['section'=2,'dp'=4,'tensor'=4] {'section','dp','tensor'}, use_global_device_ids=true, to_apply=%region_26.27 | all-reduce | flops 6147 | bytes 49176 | tf_op jit(solution)/shard_map/psum | solution.py:255
  629.4 354.8 %all-reduce.13.cloned.1.call-done = (bf16[1,2,2048,512]{3,2,1,0:T(8,128)(2,1)}, bf16[2048,688]{0,1:T(8,128)(2,1)}, bf16[2048,688]{0,1:T(8,128)(2,1)}, bf16[688,2048]{1,0:T(8,128)(2,1)}) async-done(((bf16[1,2,2048,512]{3,2,1,0:T(8,128)(2,1)}, bf16[2048,688]{0,1:T(8,128)(2,1)}, bf16[2048,688]{0,1:T(8,128)(2,1)}, bf16[688,2048]{1,0:T(8,128)(2,1)}), (bf16[1,2,2048,512]{3,2,1,0:T(8,128)(2,1)}, ...) | async-done | bytes 12648464 | tf_op jit(solution)/shard_map/psum | solution.py:245
  984.1 6.9 convert_element_type.141
  1001.1 35.9 %reduce-scatter.5.cloned.1.call-done = bf16[960,256]{1,0:T(8,128)(2,1)} async-done(((bf16[960,2048]{1,0:T(8,128)(2,1)}), bf16[960,256]{1,0:T(8,128)(2,1)}) %reduce-scatter.5.cloned.1.call-update) | async-done | bytes 491536 | tf_op jit(solution)/shard_map/reduce_scatter | solution.py:237
  (128 shorter events, 72.1 us)
Async XLA Ops:
  7.2 269.3 %copy-start = (bf16[688,2048]{1,0:T(8,128)(2,1)S(1)}, bf16[688,2048]{1,0:T(8,128)(2,1)}, u32[]{:S(2)}) copy-start(bf16[688,2048]{1,0:T(8,128)(2,1)} %param.27) | copy-start | bytes 8454148
  7.2 82.0 %all-reduce.7.cloned.1.call-start = ((), (), s32[]{:S(2)}) async-start(), calls=%async_computation.2 | async-start | bytes 3932160 | tf_op jit(solution)/shard_map/psum | solution.py:13
  27.1 231.2 %all-reduce.9.cloned.1.call-start = ((), (), s32[]{:S(2)}) async-start(), calls=%async_computation.3 | async-start | bytes 15728640 | tf_op jit(solution)/shard_map/psum | solution.py:169
  101.4 321.1 %all-reduce.11.cloned.1.call-start = ((), (), s32[]{:S(2)}) async-start(), calls=%async_computation.5 | async-start | bytes 15728640 | tf_op jit(solution)/shard_map/psum | solution.py:206
  263.8 32.6 %copy-start.2 = (f32[960,2048]{1,0:T(8,128)}, f32[960,2048]{1,0:T(8,128)S(1)}, u32[]{:S(2)}) copy-start(f32[960,2048]{1,0:T(8,128)S(1)} %get-tuple-element.85) | copy-start | bytes 23592964
  264.6 7.2 copy-start.12
  264.6 7.2 copy-start.20
  276.5 7.0 copy-start.32
  300.4 278.6 %reduce-scatter.3.cloned.1.call-start = ((), (), s32[]{:S(2)}) async-start(), calls=%async_computation.4 | async-start | bytes 4423680 | tf_op jit(solution)/shard_map/reduce_scatter | solution.py:183
  307.8 676.3 %all-reduce.13.cloned.1.call-start = ((), (), s32[]{:S(2)}) async-start(), calls=%async_computation.7 | async-start | bytes 25296896 | tf_op jit(solution)/shard_map/psum | solution.py:245
  307.9 122.5 %copy-start.9 = (bf16[2,960,512]{2,1,0:T(8,128)(2,1)S(1)}, bf16[2,960,512]{2,1,0:T(8,128)(2,1)}, u32[]{:S(2)}) copy-start(bf16[2,960,512]{2,1,0:T(8,128)(2,1)} %all-reduce.7.cloned.1.call-done) | copy-start | bytes 5898244
  438.7 9.5 copy-start.23
  438.7 9.4 copy-start.13
  438.7 9.4 copy-start.37
  438.7 106.2 %collective-permute-start = (bf16[2,960,512]{2,1,0:T(8,128)(2,1)S(1)}, bf16[2,960,512]{2,1,0:T(8,128)(2,1)S(1)}, u32[]{:S(2)}, u32[]{:S(2)}) collective-permute-start(bf16[2,960,512]{2,1,0:T(8,128)(2,1)S(1)} %get-tuple-element.70), channel_id=1, source_target_pairs={{16,0},{17,1},{18,2},{19,3},{20,4},{21,5},{22,6},{23,7},{24,8},{25... | collective-permute-start | bytes 5898248 | tf_op jit(solution)/shard_map/ppermute | solution.py:19
  452.7 92.3 %copy-start.11 = (bf16[960,2048]{1,0:T(8,128)(2,1)S(1)}, bf16[960,2048]{1,0:T(8,128)(2,1)}, u32[]{:S(2)}) copy-start(bf16[960,2048]{1,0:T(8,128)(2,1)} %copy-done.10) | copy-start | bytes 11796484
  452.7 92.3 %copy-start.24 = (bf16[960,512]{1,0:T(8,128)(2,1)S(1)}, bf16[960,512]{1,0:T(8,128)(2,1)}, u32[]{:S(2)}) copy-start(bf16[960,512]{1,0:T(8,128)(2,1)} %copy-done.23) | copy-start | bytes 2949124
  552.8 484.2 %reduce-scatter.5.cloned.1.call-start = ((), (), s32[]{:S(2)}) async-start(), calls=%async_computation.6 | async-start | bytes 4423680 | tf_op jit(solution)/shard_map/reduce_scatter | solution.py:237
  554.4 7.0 copy-start.26
  554.4 7.0 copy-start.28
  561.4 8.7 copy-start.4
  561.4 8.7 copy-start.7
  561.4 8.7 copy-start.29
  997.8 39.2 %copy-start.1 = (bf16[688,2048]{1,0:T(8,128)(2,1)S(1)}, bf16[688,2048]{1,0:T(8,128)(2,1)}, u32[]{:S(2)}) copy-start(bf16[688,2048]{1,0:T(8,128)(2,1)} %param.27) | copy-start | bytes 8454148
  (20 other events, 73.8 us)
Sparse Core Ops, SparseCore 0:
  27.3 61.8 all-reduce.6
  101.5 156.8 all-reduce.8
  300.5 121.9 all-reduce.10
  426.9 50.1 reduce-scatter.2
  552.9 431.1 all-reduce.12
  988.1 48.8 reduce-scatter.4
where the time goes:
time: 1050 us; the launch traced here: 1040 us
  waiting for transfers between devices  811 us (77%)
  matrix products  84.3 us (8%)
  other arithmetic  57.1 us (5%)
  blocking collectives  44.1 us (4%)
  between operations  16.1 us (2%)
  loops' own time  15.3 us (1%)
  local copies, waits for them, and re-layouts  14.1 us (1%)
    psum x1, waiting for transfers between devices, shards(): lax.psum(attn_weight_grad.astype(jnp.bfloat16), 'dp').astype(jnp.float32)  355 us
    psum x1, waiting for transfers between devices, shards(): branch = lax.psum(partial_branch, ('section', 'tensor'))  156 us
    psum x1, waiting for transfers between devices, shards(): lax.psum(resid_part, ('section', 'tensor'))  115 us
    ppermute x1, waiting for transfers between devices, passed_along(): lax.ppermute(value, axis, [(source, source + steps) for source in range(i...  87.8 us
    psum x1, waiting for transfers between devices, spread(): return lax.psum(kept, axis)  61.7 us
    psum x1, blocking collectives, shards(): lax.psum((gain_terms, stat_terms), ('section', 'dp', 'tensor'))  44.1 us
    reduce_scatter x1, waiting for transfers between devices, shards(): lax.psum_scatter(input_part.astype(jnp.bfloat16), ('section', 'tensor'),...  35.9 us
    dot_general x5, matrix products, contract_cols(): lax.dot_general(left_mat, right_mat, (((1,), (1,)), ((), ())), preferred_...  35.3 us
  transfers between devices with their start and end apart: 7, of which 6 were waited for; matrix products, arithmetic and copies ran while one was open for 8% of the time, Pallas kernels for 0%

commit v1 on v0

--- a/solution.py
+++ b/solution.py
@@ -242,7 +242,9 @@
     input_grad = input_sum.astype(jnp.bfloat16)
     attn_weight_grad = jnp.stack([w_first_grad, w_second_grad])[None]
     attn_weight_grad, gate_grad, up_grad, down_grad = (
-        lax.psum(attn_weight_grad.astype(jnp.bfloat16), "dp").astype(jnp.float32),
+        jnp.sum(lax.all_gather(attn_weight_grad.astype(jnp.bfloat16), "dp"), axis=0).astype(
+            jnp.float32
+        ),
         lax.psum(gate_grad.astype(jnp.bfloat16), "dp").astype(jnp.float32),
         lax.psum(up_grad.astype(jnp.bfloat16), "dp").astype(jnp.float32),
         lax.psum(down_grad.astype(jnp.bfloat16), "dp").astype(jnp.float32),

time: 1050 us -> 1130 us (1.076)
  waiting for transfers between devices: 811 us -> 871 us
  other arithmetic: 57.1 us -> 71.9 us
    all_gather x0 -> x1, waiting for transfers between devices: none -> 275 us  [shards(): lax.all_gather(attn_weight_grad.astype(jnp.bfloat16), 'dp')]
    psum x1, waiting for transfers between devices: 355 us -> 141 us  [shards(): lax.psum(gate_grad.astype(jnp.bfloat16), 'dp').astype(jnp.float32)]
    ppermute x1, waiting for transfers between devices: 87.8 us -> 107 us  [passed_along(): lax.ppermute(value, axis, [(source, source + steps) for source in range(i...]
    psum x1, waiting for transfers between devices: 115 us -> 96.9 us  [shards(): lax.psum(resid_part, ('section', 'tensor'))]
    reduce_sum x0 -> x1, other arithmetic: none -> 12.1 us  [shards(): jnp.sum(lax.all_gather(attn_weight_grad.astype(jnp.bfloat16), 'dp'), axis=0)]
  transfers between devices with their start and end apart: 7 -> 8, of which waited for: 6 -> 7; matrix products, arithmetic and copies ran while one was open for 8% -> 9% of each run, Pallas kernels for 0% -> 0%
where the time goes in v1:
time: 1130 us; the launch traced here: 1120 us
  waiting for transfers between devices  871 us (77%)
  matrix products  86.6 us (8%)
  other arithmetic  71.9 us (6%)
  blocking collectives  46.1 us (4%)
  between operations  16.4 us (1%)
  local copies, waits for them, and re-layouts  15.1 us (1%)
  loops' own time  13.1 us (1%)
    all_gather x1, waiting for transfers between devices, shards(): lax.all_gather(attn_weight_grad.astype(jnp.bfloat16), 'dp')  275 us
    psum x1, waiting for transfers between devices, shards(): branch = lax.psum(partial_branch, ('section', 'tensor'))  157 us
    psum x1, waiting for transfers between devices, shards(): lax.psum(gate_grad.astype(jnp.bfloat16), 'dp').astype(jnp.float32)  141 us
    ppermute x1, waiting for transfers between devices, passed_along(): lax.ppermute(value, axis, [(source, source + steps) for source in range(i...  107 us
    psum x1, waiting for transfers between devices, shards(): lax.psum(resid_part, ('section', 'tensor'))  96.9 us
    psum x1, waiting for transfers between devices, spread(): return lax.psum(kept, axis)  61.7 us
    psum x1, blocking collectives, shards(): lax.psum((gain_terms, stat_terms), ('section', 'dp', 'tensor'))  46.1 us
    dot_general x5, matrix products, contract_cols(): lax.dot_general(left_mat, right_mat, (((1,), (1,)), ((), ())), preferred_...  35.6 us
  transfers between devices with their start and end apart: 8, of which 7 were waited for; matrix products, arithmetic and copies ran while one was open for 9% of the time, Pallas kernels for 0%

profile of v1, /device:TPU:0, one launch (start us, length us, event | category | flops | bytes accessed | tf_op | source)
XLA Modules:
  0.0 1121.9 jit_solution(2338763219628456113)
XLA Ops:
  27.5 61.7 %all-reduce.7.cloned.1.call-done = bf16[2,960,512]{2,1,0:T(8,128)(2,1)} async-done(((bf16[2,960,512]{2,1,0:T(8,128)(2,1)}), bf16[2,960,512]{2,1,0:T(8,128)(2,1)}) %all-reduce.7.cloned.1.call-update) | async-done | bytes 1966096 | tf_op jit(solution)/shard_map/psum | solution.py:13
  89.2 7.8 conditional.6
  101.9 156.8 %all-reduce.9.cloned.1.call-done = f32[960,2048]{1,0:T(8,128)} async-done(((f32[960,2048]{1,0:T(8,128)}), f32[960,2048]{1,0:T(8,128)}) %all-reduce.9.cloned.1.call-update) | async-done | bytes 7864336 | tf_op jit(solution)/shard_map/psum | solution.py:169
  258.6 5.4 multiply_reduce_fusion.3
  264.9 7.2 fusion.81
  276.8 7.4 multiply_convert_fusion.4
  289.6 7.5 multiply_reduce_fusion.1
  301.1 7.3 add_convert_fusion
  309.8 6.8 convolution_convert_fusion.2
  325.6 96.9 %all-reduce.11.cloned.1.call-done = f32[960,2048]{1,0:T(8,128)} async-done(((f32[960,2048]{1,0:T(8,128)}), f32[960,2048]{1,0:T(8,128)}) %all-reduce.11.cloned.1.call-update) | async-done | bytes 7864336 | tf_op jit(solution)/shard_map/psum | solution.py:206
  422.5 7.8 fusion.51
  430.4 6.2 conditional.8
  437.9 107.3 %collective-permute-done = bf16[2,960,512]{2,1,0:T(8,128)(2,1)S(1)} collective-permute-done((bf16[2,960,512]{2,1,0:T(8,128)(2,1)S(1)}, bf16[2,960,512]{2,1,0:T(8,128)(2,1)S(1)}, u32[]{:S(2)}, u32[]{:S(2)}) %collective-permute-start) | collective-permute-done | bytes 1966112 | tf_op jit(solution)/shard_map/ppermute | solution.py:19
  545.2 5.5 fusion.59
  557.3 7.1 conditional.9
  557.3 6.8 fusion.38
  564.5 8.6 fusion.50
  573.1 6.9 fusion.47
  585.8 46.1 %all-reduce = (f32[3,2048]{1,0:T(4,128)S(1)}, f32[3]{0:T(128)S(1)}) all-reduce(f32[3,2048]{1,0:T(4,128)S(1)} %pad_maximum_fusion.2, f32[3]{0:T(128)S(1)} %pad_maximum_fusion.3), channel_id=1, replica_groups=mesh['section'=2,'dp'=4,'tensor'=4] {'section','dp','tensor'}, use_global_device_ids=true, to_apply=%region_26.27 | all-reduce | flops 6147 | bytes 49176 | tf_op jit(solution)/shard_map/psum | solution.py:257
  634.3 140.7 %all-reduce.13.cloned.1.call-done = (bf16[2048,688]{0,1:T(8,128)(2,1)}, bf16[2048,688]{0,1:T(8,128)(2,1)}, bf16[688,2048]{1,0:T(8,128)(2,1)}) async-done(((bf16[2048,688]{0,1:T(8,128)(2,1)}, bf16[2048,688]{0,1:T(8,128)(2,1)}, bf16[688,2048]{1,0:T(8,128)(2,1)}), (bf16[2048,688]{0,1:T(8,128)(2,1)}, bf16[2048,688]{0,1:T(8,128)(2,1)}, bf16[688,2048]{1,0:T(8,128)(2,1)})) %all-reduce.13.cloned.1.call-update) | async-done | bytes 8454160 | tf_op jit(solution)/shard_map/psum | solution.py:248
  787.6 274.7 %all-gather.2.cloned.1.call-done = bf16[4,1,2,2048,512]{4,3,2,1,0:T(8,128)(2,1)} async-done(((bf16[1,1,2,2048,512]{4,3,2,1,0:T(8,128)(2,1)}), bf16[4,1,2,2048,512]{4,3,2,1,0:T(8,128)(2,1)}) %all-gather.2.cloned.1.call-update) | async-done | bytes 16777232 | tf_op jit(solution)/shard_map/all_gather | solution.py:245
  1062.2 12.1 %reduce_sum.127 = bf16[2,2048,512]{2,1,0:T(8,128)(2,1)} reduce(bf16[4,1,2,2048,512]{4,3,2,1,0:T(8,128)(2,1)} %all-gather.2.cloned.1.call-done, bf16[]{:T(256)} %constant.37.clone.1), dimensions={0,1}, to_apply=%region_27.28 | reduce | flops 6291456 | bytes 20971522 | tf_op jit(solution)/shard_map/reduce_sum | solution.py:245
  1074.4 7.2 bitcast_convert_fusion
  1081.5 33.0 %reduce-scatter.5.cloned.1.call-done = bf16[960,256]{1,0:T(8,128)(2,1)} async-done(((bf16[960,2048]{1,0:T(8,128)(2,1)}), bf16[960,256]{1,0:T(8,128)(2,1)}) %reduce-scatter.5.cloned.1.call-update) | async-done | bytes 491536 | tf_op jit(solution)/shard_map/reduce_scatter | solution.py:237
  (130 shorter events, 87.7 us)
Async XLA Ops:
  7.2 269.6 %copy-start = (bf16[688,2048]{1,0:T(8,128)(2,1)S(1)}, bf16[688,2048]{1,0:T(8,128)(2,1)}, u32[]{:S(2)}) copy-start(bf16[688,2048]{1,0:T(8,128)(2,1)} %param.27) | copy-start | bytes 8454148
  7.2 82.0 %all-reduce.7.cloned.1.call-start = ((), (), s32[]{:S(2)}) async-start(), calls=%async_computation.2 | async-start | bytes 3932160 | tf_op jit(solution)/shard_map/psum | solution.py:13
  7.3 6.8 copy-start.3
  27.1 231.5 %all-reduce.9.cloned.1.call-start = ((), (), s32[]{:S(2)}) async-start(), calls=%async_computation.3 | async-start | bytes 15728640 | tf_op jit(solution)/shard_map/psum | solution.py:169
  101.2 321.3 %all-reduce.11.cloned.1.call-start = ((), (), s32[]{:S(2)}) async-start(), calls=%async_computation.5 | async-start | bytes 15728640 | tf_op jit(solution)/shard_map/psum | solution.py:206
  264.1 33.0 %copy-start.2 = (f32[960,2048]{1,0:T(8,128)}, f32[960,2048]{1,0:T(8,128)S(1)}, u32[]{:S(2)}) copy-start(f32[960,2048]{1,0:T(8,128)S(1)} %get-tuple-element.84) | copy-start | bytes 23592964
  264.8 7.2 copy-start.12
  264.9 7.2 copy-start.20
  276.8 7.4 copy-start.31
  301.0 281.0 %reduce-scatter.3.cloned.1.call-start = ((), (), s32[]{:S(2)}) async-start(), calls=%async_computation.4 | async-start | bytes 4423680 | tf_op jit(solution)/shard_map/reduce_scatter | solution.py:183
  308.4 8.2 copy-start.36
  308.4 466.6 %all-reduce.13.cloned.1.call-start = ((), (), s32[]{:S(2)}) async-start(), calls=%async_computation.8 | async-start | bytes 16908288 | tf_op jit(solution)/shard_map/psum | solution.py:248
  309.7 6.8 copy-start.13
  325.5 736.7 %all-gather.2.cloned.1.call-start = ((), (), s32[]{:S(2)}) async-start(), calls=%async_computation.7 | async-start | bytes 20971520 | tf_op jit(solution)/shard_map/all_gather | solution.py:245
  325.6 104.8 %copy-start.9 = (bf16[2,960,512]{2,1,0:T(8,128)(2,1)S(1)}, bf16[2,960,512]{2,1,0:T(8,128)(2,1)}, u32[]{:S(2)}) copy-start(bf16[2,960,512]{2,1,0:T(8,128)(2,1)} %all-reduce.7.cloned.1.call-done) | copy-start | bytes 5898244
  436.6 108.6 %copy-start.23 = (bf16[960,512]{1,0:T(8,128)(2,1)}, bf16[960,512]{1,0:T(8,128)(2,1)S(1)}, u32[]{:S(2)}) copy-start(bf16[960,512]{1,0:T(8,128)(2,1)S(1)} %get-tuple-element.71) | copy-start | bytes 2949124
  436.6 108.6 %collective-permute-start = (bf16[2,960,512]{2,1,0:T(8,128)(2,1)S(1)}, bf16[2,960,512]{2,1,0:T(8,128)(2,1)S(1)}, u32[]{:S(2)}, u32[]{:S(2)}) collective-permute-start(bf16[2,960,512]{2,1,0:T(8,128)(2,1)S(1)} %get-tuple-element.70), channel_id=1, source_target_pairs={{16,0},{17,1},{18,2},{19,3},{20,4},{21,5},{22,6},{23,7},{24,8},{25... | collective-permute-start | bytes 5898248 | tf_op jit(solution)/shard_map/ppermute | solution.py:19
  555.8 558.8 %reduce-scatter.5.cloned.1.call-start = ((), (), s32[]{:S(2)}) async-start(), calls=%async_computation.6 | async-start | bytes 4423680 | tf_op jit(solution)/shard_map/reduce_scatter | solution.py:237
  557.3 7.1 copy-start.25
  557.3 7.1 copy-start.27
  564.4 8.7 copy-start.4
  564.4 8.7 copy-start.7
  564.5 8.7 copy-start.28
  1062.2 52.4 %copy-start.1 = (bf16[688,2048]{1,0:T(8,128)(2,1)S(1)}, bf16[688,2048]{1,0:T(8,128)(2,1)}, u32[]{:S(2)}) copy-start(bf16[688,2048]{1,0:T(8,128)(2,1)} %param.27) | copy-start | bytes 8454148
  (20 other events, 74.5 us)
Sparse Core Ops, SparseCore 0:
  27.3 61.8 all-reduce.6
  101.3 157.2 all-reduce.8
  301.1 121.3 all-reduce.10
  426.9 50.1 reduce-scatter.2
  479.7 295.2 all-reduce.12
  776.5 285.7 all-gather.1
  1066.3 48.2 reduce-scatter.4
